TPU v7x, 32 devices: a whole 2x2x4 slice. The times are simulated.
32 devices in a mesh: cuts: 2 (over y), ctx: 16 (over z, x, core).
Axes of the slice: x: 2, y: 2, z: 4, core: 2. Of those that a mesh axis runs over, the one named last changes fastest.
Arguments:
- queries: bfloat16 [4096, 8192], P('ctx')
- keys: bfloat16 [4096, 1024], P(('cuts', 'ctx'))
- values: bfloat16 [4096, 1024], P(('cuts', 'ctx')), may hold values from -6 to 6
- bounds: int32 [3, 32], replicated, may hold values from 0 to 31, as said below
Outputs:
- attended: bfloat16 [4096, 8192], P('ctx', 'cuts')
Inputs may be any that keep to these rules, and one draw needn't show every extreme that they name: The sequence is a row of trees laid end to end in whole mask blocks: each tree is a prompt of 1 to 4 mask blocks followed by up to 8 responses of 1 to 2 mask blocks each, so a tree spans at most 20 mask blocks; the last mask block is a one-block prompt of its own, and the tree before it may be cut off. For a block b of a prompt, bounds[0, b] is the prompt's first block and bounds[1, b] = bounds[2, b] = bounds[0, b]; for a block of a response, bounds[0, b] is the response's first block and bounds[1, b] < bounds[2, b] <= bounds[0, b] delimit the prompt of its tree. Block 0 starts a prompt.
All inputs are finite; a program needn't handle non-finite values.
Results may differ from a plain program's by a relative error of at most 0.014.
Values may be sent and summed in bfloat16 or wider, within the bound.
No kernel may reach another device: no remote copies, remote signals or barrier semaphores. Data moves between devices by JAX's collectives and lax.ppermute only.
A program may use at most 64 MiB of HBM per device.

v0:
```python
import functools

import jax
import jax.numpy as jnp
from jax import lax
from jax.experimental import pallas as pl
from jax.experimental.pallas import tpu as pltpu
from jax.sharding import PartitionSpec as P

QUERY_HEADS = 64
KEY_VALUE_HEADS = 8
HEAD_SIZE = 128
GROUP_SIZE = QUERY_HEADS // KEY_VALUE_HEADS
BLK = 128
PROMPT_BLOCKS = 4
REPLY_BLOCKS = 2
MOST_BLOCKS = PROMPT_BLOCKS + REPLY_BLOCKS
NEGATIVE_FILL = -1e30
EXP2_SCALE = 1.4426950408889634 * HEAD_SIZE ** (-0.5)
VMEM_LIMIT = 48 * 1024 * 1024


def attend(count, query_ref, keys_now, values_now, out_ref):
    width = count * BLK
    keys = keys_now[0:width, :]
    values = values_now[0:width, :]
    row = lax.broadcasted_iota(jnp.int32, (BLK, BLK), 0)
    column = lax.broadcasted_iota(jnp.int32, (BLK, BLK), 1)
    causal = column <= row
    for head in range(GROUP_SIZE):
        span = slice(head * HEAD_SIZE, (head + 1) * HEAD_SIZE)
        score = lax.dot_general(
            query_ref[:, span], keys, (((1,), (1,)), ((), ())), preferred_element_type=jnp.float32
        )
        parts = [score[:, i * BLK : (i + 1) * BLK] for i in range(count)]
        parts[-1] = jnp.where(causal, parts[-1], NEGATIVE_FILL)
        peak = functools.reduce(jnp.maximum, parts)
        peak = jnp.max(peak, axis=1, keepdims=True)
        weight = [jnp.exp2((part - peak) * EXP2_SCALE).astype(jnp.bfloat16) for part in parts]
        weight = weight[0] if count == 1 else jnp.concatenate(weight, axis=1)
        both = jnp.dot(weight, values, preferred_element_type=jnp.float32)
        result = both[:, :HEAD_SIZE] / both[:, HEAD_SIZE:]
        out_ref[:, span] = result.astype(out_ref.dtype)


def attention_kernel(slot_of, place_ref, bounds_ref, query_ref, kv_ref, out_ref, keys_now, values_now):
    q_id = pl.program_id(0)
    head = pl.program_id(1)
    block = place_ref[0] + q_id
    own = bounds_ref[0, block]
    first = bounds_ref[1, block]
    prompt = bounds_ref[2, block] - first
    count = prompt + block - own + 1
    column = pl.multiple_of(head * HEAD_SIZE, HEAD_SIZE)

    @pl.when((q_id == 0) & (head == 0))
    def _():
        values_now[:, HEAD_SIZE:] = jnp.ones((values_now.shape[0], HEAD_SIZE), values_now.dtype)

    for i in range(MOST_BLOCKS):

        @pl.when(i < count)
        def _():
            which = jnp.where(i < prompt, first + i, own + i - prompt)
            slot = slot_of(place_ref, which)
            keys_now[i * BLK : (i + 1) * BLK, :] = kv_ref[slot, 0, :, pl.ds(column, HEAD_SIZE)]
            values_now[i * BLK : (i + 1) * BLK, :HEAD_SIZE] = kv_ref[
                slot, 1, :, pl.ds(column, HEAD_SIZE)
            ]

    for n in range(1, MOST_BLOCKS + 1):

        @pl.when(count == n)
        def _():
            attend(n, query_ref, keys_now, values_now, out_ref)


def attention(queries, kv, bounds, place, slot_of, heads_here):
    rows = queries.shape[0]
    kv_heads = heads_here // GROUP_SIZE
    wide = GROUP_SIZE * HEAD_SIZE
    grid_spec = pltpu.PrefetchScalarGridSpec(
        num_scalar_prefetch=2,
        grid=(rows // BLK, kv_heads),
        in_specs=[
            pl.BlockSpec((BLK, wide), lambda q, g, place, bounds: (q, place[1] * kv_heads + g)),
            pl.BlockSpec(kv.shape, lambda q, g, place, bounds: (0, 0, 0, 0)),
        ],
        out_specs=pl.BlockSpec((BLK, wide), lambda q, g, place, bounds: (q, g)),
        scratch_shapes=[
            pltpu.VMEM((MOST_BLOCKS * BLK, HEAD_SIZE), jnp.bfloat16),
            pltpu.VMEM((MOST_BLOCKS * BLK, 2 * HEAD_SIZE), jnp.bfloat16),
        ],
    )
    return pl.pallas_call(
        functools.partial(attention_kernel, slot_of),
        grid_spec=grid_spec,
        out_shape=jax.ShapeDtypeStruct((rows, heads_here * HEAD_SIZE), jnp.bfloat16),
        compiler_params=pltpu.CompilerParams(vmem_limit_bytes=VMEM_LIMIT),
        name="attention",
    )(place, bounds, queries, kv)


def gathered_local(cuts, queries, keys, values, bounds):
    heads_here = QUERY_HEADS // cuts
    columns = KEY_VALUE_HEADS * HEAD_SIZE // cuts
    rows = keys.shape[0]
    both = jnp.stack([keys, values], 0).reshape(2, rows, cuts, columns)
    both = lax.all_to_all(both.transpose(2, 0, 1, 3), "cuts", 0, 0)
    both = lax.all_gather(both, "ctx", axis=0)
    both = both.transpose(2, 1, 0, 3, 4).reshape(2, -1, BLK, columns).transpose(1, 0, 2, 3)
    place = jnp.stack([lax.axis_index("ctx") * (queries.shape[0] // BLK), lax.axis_index("cuts")])
    return attention(queries, both, bounds, place, lambda place_ref, which: which, heads_here)


def solution(mesh):
    cuts = mesh.shape["cuts"]
    in_specs = (P("ctx", None), P(("cuts", "ctx"), None), P(("cuts", "ctx"), None), P())
    out_specs = P("ctx", "cuts")
    local = functools.partial(gathered_local, cuts)
    return jax.shard_map(local, mesh=mesh, in_specs=in_specs, out_specs=out_specs, check_vma=False)
```

profile of v0, /device:TPU:13, one launch (start us, length us, event | category | flops | bytes accessed | tf_op | source)
XLA Modules:
  0.0 127.4 jit_solution(16595387066354710759)
XLA Ops:
  6.5 0.0 all-gather.3.cloned.1.call-start
  6.5 1.1 copy.15
  7.7 1.1 copy.16
  8.8 0.1 maximum_bitcast_fusion
  8.9 8.7 %all_to_all.5 = bf16[2,2,128,512]{2,3,1,0:T(8,128)(2,1)S(1)} all-to-all(bf16[2,2,128,512]{2,3,1,0:T(8,128)(2,1)S(1)} %copy.17), channel_id=1, replica_groups=mesh['cuts'=2,'ctx'=16] {'cuts'}, dimensions={0} | all-to-all | bytes 1048576 | tf_op jit(solution)/shard_map/all_to_all | solution.py:109
  17.6 1.0 copy.18
  18.6 0.0 all-gather.3.cloned.1.call-update
  18.6 0.1 pad_add_fusion.place_ref
  18.7 76.9 %all-gather.3.cloned.1.call-done = bf16[32,2,128,512]{3,2,1,0:T(8,128)(2,1)} async-done(((bf16[2,2,128,512]{3,2,1,0:T(8,128)(2,1)}), bf16[32,2,128,512]{3,2,1,0:T(8,128)(2,1)}) %all-gather.3.cloned.1.call-update) | async-done | bytes 8388624 | tf_op jit(solution)/shard_map/all_gather | solution.py:110
  95.6 0.0 copy-start
  95.6 0.0 copy-start.1
  95.6 7.7 %copy.19 = bf16[2,2,16,128,512]{4,3,0,2,1:T(8,128)(2,1)} copy(bf16[2,2,16,128,512]{4,3,0,1,2:T(8,128)(2,1)} %bitcast.13) | data formatting | bytes 16777216 | tf_op jit(solution)/shard_map/transpose | solution.py:111
  103.4 0.0 copy-done
  103.4 0.0 copy-done.1
  103.4 17.2 %attention.1 = bf16[256,4096]{1,0:T(8,128)(2,1)} custom-call(s32[2]{0:T(128)S(1)} %pad_add_fusion.place_ref, s32[3,32]{1,0:T(4,128)S(1)} %copy-done.1, bf16[256,8192]{1,0:T(8,128)(2,1)S(1)} %copy-done, bf16[32,2,128,512]{3,2,1,0:T(8,128)(2,1)} %bitcast.12), custom_call_target="tpu_custom_call" | custom-call | tf_op jit(solution)/shard_map/attention/pallas_call | solution.py:95
  (1 shorter events, 0.0 us)
Async XLA Ops:
  6.5 89.1 %all-gather.3.cloned.1.call-start = ((), (), s32[]{:S(2)}) async-start(), calls=%async_computation.1 | async-start | bytes 8912896 | tf_op jit(solution)/shard_map/all_gather | solution.py:110
  95.6 7.8 %copy-start = (bf16[256,8192]{1,0:T(8,128)(2,1)S(1)}, bf16[256,8192]{1,0:T(8,128)(2,1)}, u32[]{:S(2)}) copy-start(bf16[256,8192]{1,0:T(8,128)(2,1)} %query_ref.1) | copy-start | bytes 12582916
  95.6 7.8 %copy-start.1 = (s32[3,32]{1,0:T(4,128)S(1)}, s32[3,32]{1,0:T(4,128)}, u32[]{:S(2)}) copy-start(s32[3,32]{1,0:T(4,128)} %bounds_ref.1) | copy-start | bytes 1156
Sparse Core Ops, SparseCore 0:
  18.7 76.8 all-gather.2
where the time goes:
time: 130 us; the launch traced here: 127 us
  waiting for transfers between devices  76.9 us (59%)
  Pallas kernels  17.2 us (13%)
  between operations  13.4 us (10%)
  local copies, waits for them, and re-layouts  11 us (8%)
  blocking collectives  8.7 us (7%)
    all_gather x1, waiting for transfers between devices, gathered_local(): both = lax.all_gather(both, 'ctx', axis=0)  76.9 us
    pallas_call x1, Pallas kernels, attention(): pl.pallas_call(functools.partial(attention_kernel, slot_of), grid_spec=gr...  17.2 us
    all_to_all x1, blocking collectives, gathered_local(): both = lax.all_to_all(both.transpose(2, 0, 1, 3), 'cuts', 0, 0)  8.7 us
    transpose x1, local copies, waits for them, and re-layouts, gathered_local(): both.transpose(2, 1, 0, 3, 4).reshape(2, -1, BLK, columns)  7.74 us
  transfers between devices with their start and end apart: 1, of which 1 were waited for; matrix products, arithmetic and copies ran while one was open for 0% of the time, Pallas kernels for 0%

commit v1 on v0

--- a/solution.py
+++ b/solution.py
@@ -15,6 +15,7 @@
 PROMPT_BLOCKS = 4
 REPLY_BLOCKS = 2
 MOST_BLOCKS = PROMPT_BLOCKS + REPLY_BLOCKS
+CHIP_BLOCKS = 4
 NEGATIVE_FILL = -1e30
 EXP2_SCALE = 1.4426950408889634 * HEAD_SIZE ** (-0.5)
 VMEM_LIMIT = 48 * 1024 * 1024
@@ -43,9 +44,12 @@
         out_ref[:, span] = result.astype(out_ref.dtype)
 
 
-def attention_kernel(slot_of, place_ref, bounds_ref, query_ref, kv_ref, out_ref, keys_now, values_now):
+def attention_kernel(slot_of, sources, place_ref, bounds_ref, query_ref, *refs):
+    kv_refs = refs[: len(sources)]
+    out_ref, kv_now, keys_now, values_now, arrived = refs[len(sources) :]
     q_id = pl.program_id(0)
     head = pl.program_id(1)
+    chip = place_ref[0] // CHIP_BLOCKS
     block = place_ref[0] + q_id
     own = bounds_ref[0, block]
     first = bounds_ref[1, block]
@@ -55,16 +59,24 @@
 
     @pl.when((q_id == 0) & (head == 0))
     def _():
+        copies = [
+            pltpu.make_async_copy(kv_ref, kv_now.at[pl.ds(slot(place_ref), kv_ref.shape[0])], arrived.at[i])
+            for i, (kv_ref, slot) in enumerate(zip(kv_refs, sources))
+        ]
+        for copy in copies:
+            copy.start()
         values_now[:, HEAD_SIZE:] = jnp.ones((values_now.shape[0], HEAD_SIZE), values_now.dtype)
+        for copy in copies:
+            copy.wait()
 
     for i in range(MOST_BLOCKS):
 
         @pl.when(i < count)
         def _():
             which = jnp.where(i < prompt, first + i, own + i - prompt)
-            slot = slot_of(place_ref, which)
-            keys_now[i * BLK : (i + 1) * BLK, :] = kv_ref[slot, 0, :, pl.ds(column, HEAD_SIZE)]
-            values_now[i * BLK : (i + 1) * BLK, :HEAD_SIZE] = kv_ref[
+            slot = slot_of(bounds_ref, chip, which)
+            keys_now[i * BLK : (i + 1) * BLK, :] = kv_now[slot, 0, :, pl.ds(column, HEAD_SIZE)]
+            values_now[i * BLK : (i + 1) * BLK, :HEAD_SIZE] = kv_now[
                 slot, 1, :, pl.ds(column, HEAD_SIZE)
             ]
 
@@ -75,30 +87,30 @@
             attend(n, query_ref, keys_now, values_now, out_ref)
 
 
-def attention(queries, kv, bounds, place, slot_of, heads_here):
+def attention(queries, kv, sources, slots, bounds, place, slot_of, heads_here):
     rows = queries.shape[0]
     kv_heads = heads_here // GROUP_SIZE
     wide = GROUP_SIZE * HEAD_SIZE
     grid_spec = pltpu.PrefetchScalarGridSpec(
         num_scalar_prefetch=2,
         grid=(rows // BLK, kv_heads),
-        in_specs=[
-            pl.BlockSpec((BLK, wide), lambda q, g, place, bounds: (q, place[1] * kv_heads + g)),
-            pl.BlockSpec(kv.shape, lambda q, g, place, bounds: (0, 0, 0, 0)),
-        ],
+        in_specs=[pl.BlockSpec((BLK, wide), lambda q, g, place, bounds: (q, place[1] * kv_heads + g))]
+        + [pl.BlockSpec(memory_space=pl.ANY)] * len(kv),
         out_specs=pl.BlockSpec((BLK, wide), lambda q, g, place, bounds: (q, g)),
         scratch_shapes=[
+            pltpu.VMEM((slots,) + kv[0].shape[1:], jnp.bfloat16),
             pltpu.VMEM((MOST_BLOCKS * BLK, HEAD_SIZE), jnp.bfloat16),
             pltpu.VMEM((MOST_BLOCKS * BLK, 2 * HEAD_SIZE), jnp.bfloat16),
+            pltpu.SemaphoreType.DMA((len(kv),)),
         ],
     )
     return pl.pallas_call(
-        functools.partial(attention_kernel, slot_of),
+        functools.partial(attention_kernel, slot_of, sources),
         grid_spec=grid_spec,
         out_shape=jax.ShapeDtypeStruct((rows, heads_here * HEAD_SIZE), jnp.bfloat16),
         compiler_params=pltpu.CompilerParams(vmem_limit_bytes=VMEM_LIMIT),
         name="attention",
-    )(place, bounds, queries, kv)
+    )(place, bounds, queries, *kv)
 
 
 def gathered_local(cuts, queries, keys, values, bounds):
@@ -110,12 +122,200 @@
     both = lax.all_gather(both, "ctx", axis=0)
     both = both.transpose(2, 1, 0, 3, 4).reshape(2, -1, BLK, columns).transpose(1, 0, 2, 3)
     place = jnp.stack([lax.axis_index("ctx") * (queries.shape[0] // BLK), lax.axis_index("cuts")])
-    return attention(queries, both, bounds, place, lambda place_ref, which: which, heads_here)
+    sources = [lambda place_ref: 0]
+    return attention(
+        queries, [both], sources, both.shape[0], bounds, place, lambda b, chip, which: which, heads_here
+    )
+
+
+def crossing(bounds_ref, edge):
+    own, first, last = bounds_ref[0, edge], bounds_ref[1, edge], bounds_ref[2, edge]
+    reply = first < last
+    return jnp.where(reply, first, own), jnp.where(reply, last, edge)
+
+
+def crossing_block(bounds_ref, edge, residue):
+    low, high = crossing(bounds_ref, edge)
+    which = low + lax.rem(residue - lax.rem(low, 4) + 4, 4)
+    return jnp.where(which < high, which, -1)
+
+
+def tree_slot(bounds_ref, chip, which):
+    edge = chip * CHIP_BLOCKS
+    low, high = crossing(bounds_ref, edge)
+    crosses = (which >= low) & (which < high)
+    early = jnp.where(crosses, 4 + lax.rem(which, 4), 8)
+    return jnp.where(which >= edge, which - edge, early)
+
+
+def pick_kernel(rule, n_in, place_ref, bounds_ref, *refs):
+    ins, outs, done = refs[:n_in], refs[n_in:-1], refs[-1]
+    choices = rule(place_ref, bounds_ref)
+    for o, choice in enumerate(choices):
+        for i, in_ref in enumerate(ins):
+
+            @pl.when(choice == i)
+            def _():
+                pltpu.make_async_copy(in_ref, outs[o], done.at[o]).start()
+
+    for o in range(len(choices)):
+        pltpu.make_async_copy(ins[0], outs[o], done.at[o]).wait()
+
+
+def pick(rule, n_out, place, bounds, *arrays):
+    shape = jax.ShapeDtypeStruct(arrays[0].shape, arrays[0].dtype)
+    grid_spec = pltpu.PrefetchScalarGridSpec(
+        num_scalar_prefetch=2,
+        grid=(1,),
+        in_specs=[pl.BlockSpec(memory_space=pl.ANY)] * len(arrays),
+        out_specs=[pl.BlockSpec(memory_space=pltpu.VMEM)] * n_out,
+        scratch_shapes=[pltpu.SemaphoreType.DMA((n_out,))],
+    )
+    return pl.pallas_call(
+        functools.partial(pick_kernel, rule, len(arrays)),
+        grid_spec=grid_spec,
+        out_shape=[shape] * n_out,
+        name="pick",
+    )(place, bounds, *arrays)
+
+
+def halves_kernel(place_ref, keys_ref, values_ref, own_ref, other_ref, done):
+    cut = place_ref[1]
+    columns = own_ref.shape[3]
+    copies = []
+    for i, in_ref in enumerate((keys_ref, values_ref)):
+        for j, (out_ref, which) in enumerate(((own_ref, cut), (other_ref, 1 - cut))):
+            span = pl.ds(pl.multiple_of(which * columns, columns), columns)
+            copies.append(pltpu.make_async_copy(in_ref.at[:, span], out_ref.at[0, i], done.at[2 * i + j]))
+    for copy in copies:
+        copy.start()
+    for copy in copies:
+        copy.wait()
+
+
+def halves(place, keys, values):
+    rows, columns = keys.shape
+    shape = jax.ShapeDtypeStruct((1, 2, rows, columns // 2), keys.dtype)
+    grid_spec = pltpu.PrefetchScalarGridSpec(
+        num_scalar_prefetch=1,
+        grid=(1,),
+        in_specs=[pl.BlockSpec(memory_space=pl.ANY)] * 2,
+        out_specs=[pl.BlockSpec(memory_space=pltpu.VMEM)] * 2,
+        scratch_shapes=[pltpu.SemaphoreType.DMA((4,))],
+    )
+    return pl.pallas_call(halves_kernel, grid_spec=grid_spec, out_shape=[shape] * 2, name="halves")(
+        place, keys, values
+    )
+
+
+def where(*cases):
+    value = cases[-1]
+    for condition, choice in reversed(cases[:-1]):
+        value = jnp.where(condition, choice, value)
+    return value
+
+
+def position(place_ref):
+    ctx = place_ref[0] // 2
+    return ctx // 4, lax.rem(ctx, 4), lax.rem(ctx // 2, 2)
+
+
+def rule_spread(place_ref, bounds_ref):
+    plane, _, _ = position(place_ref)
+    cut = place_ref[1]
+    low, high = cut, 1 - cut
+    return low, where((plane == 0, low), high), where((plane == 3, low), high)
+
+
+def rule_middle(place_ref, bounds_ref):
+    plane, residue, x = position(place_ref)
+    low, high, down, up, far = 0, 1, 2, 3, 4
+    to_2 = crossing_block(bounds_ref, 16, residue)
+    to_3 = crossing_block(bounds_ref, 24, residue)
+    ahead = where(
+        (plane == 1, jnp.where(to_2 < 4, up, low)),
+        (plane == 2, where((to_3 < 12, low), (to_3 < 16, down), (to_3 < 20, far), up)),
+        low,
+    )
+    lower = where((plane == 0, low), (plane == 1, down), (plane == 2, far), up)
+    upper = where((plane == 0, down), (plane == 1, far), (plane == 2, up), high)
+    kept = jnp.where(x == 0, lower, upper)
+    sent = jnp.where(x == 0, upper, lower)
+    before = where((plane == 1, low), (plane == 2, down), (plane == 3, far), low)
+    return ahead, kept, sent, before
+
+
+def rule_last(place_ref, bounds_ref):
+    plane, residue, x = position(place_ref)
+    low, down, up, kept, sent, crossed, rare, before = 0, 1, 2, 3, 4, 5, 6, 7
+    block = crossing_block(bounds_ref, plane * 8, residue)
+    into_plane = where(
+        (plane == 1, jnp.where(block < 4, up, low)),
+        (plane == 2, where((block < 8, crossed), (block < 12, low), down)),
+        (plane == 3, jnp.where(block < 8, rare, crossed)),
+        low,
+    )
+    middle = crossing_block(bounds_ref, plane * 8 + 4, residue)
+    into_half = jnp.where(middle >= plane * 8, jnp.where(x == 0, kept, sent), into_plane)
+    mine = jnp.where(x == 0, into_plane, into_half)
+    other = jnp.where(x == 0, into_half, into_plane)
+    return mine, other, jnp.where(x == 0, before, sent)
+
+
+def tree_local(queries, keys, values, bounds):
+    heads_here = QUERY_HEADS // 2
+    place = jnp.stack([lax.axis_index("ctx") * 2, lax.axis_index("cuts")])
+    own, other = halves(place, keys, values)
+    other = lax.ppermute(other, "cuts", [(0, 1), (1, 0)])
+
+    def move(array, planes, residues=range(4)):
+        pairs = [(4 * a + r, 4 * b + r) for a, b, only in planes for r in (only or residues)]
+        return lax.ppermute(array, "ctx", pairs)
+
+    send_down, send_up, send_far = pick(rule_spread, 3, place, bounds, own, other)
+    down = move(send_down, [(1, 0, None), (2, 1, None), (3, 2, None)])
+    up = move(send_up, [(0, 1, None), (1, 2, None), (2, 3, None)])
+    far = move(send_far, [(3, 1, None), (0, 2, None), (1, 3, (3,))])
+    low = send_down
+    ahead, kept, sent, before = pick(rule_middle, 4, place, bounds, low, send_up, down, up, far)
+    crossed = move(ahead, [(1, 2, None), (2, 3, None)])
+    low_24 = jnp.where(bounds[1, 24] < bounds[2, 24], bounds[1, 24], bounds[0, 24])
+    rare = lax.cond(low_24 < 8, lambda: move(low, [(1, 3, None)]), lambda: crossed)
+    across = [(c, c ^ 2) for c in range(16)]
+    beside = [(c, c ^ 1) for c in range(16)]
+    home_x = lax.ppermute(sent, "ctx", across)
+    before_x = lax.ppermute(before, "ctx", [(4 * z + 3, 4 * z + 1) for z in range(1, 4)])
+    mine, forward, before = pick(
+        rule_last, 3, place, bounds, low, down, up, kept, sent, crossed, rare, before_x
+    )
+    far_x = lax.ppermute(forward, "ctx", across)
+    before_k = lax.ppermute(before, "ctx", [(c, c ^ 1) for c in range(1, 16, 2)])
+    kv = [kept, home_x, mine, far_x]
+    kv += [lax.ppermute(array, "ctx", beside) for array in kv]
+
+    def slot(base, flip, place_ref):
+        return base + (position(place_ref)[1] ^ flip)
+
+    sources = [
+        functools.partial(slot, base, flip ^ core)
+        for core in (0, 1)
+        for base, flip in ((0, 0), (0, 2), (4, 0), (4, 2))
+    ]
+    kv += [before, before_k]
+    sources += [lambda p: 9 - lax.rem(p[0] // 2, 2), lambda p: 8 + lax.rem(p[0] // 2, 2)]
+    return attention(queries, kv, sources, 10, bounds, place, tree_slot, heads_here)
 
 
 def solution(mesh):
-    cuts = mesh.shape["cuts"]
+    cuts, ctx = mesh.shape["cuts"], mesh.shape["ctx"]
     in_specs = (P("ctx", None), P(("cuts", "ctx"), None), P(("cuts", "ctx"), None), P())
     out_specs = P("ctx", "cuts")
-    local = functools.partial(gathered_local, cuts)
-    return jax.shard_map(local, mesh=mesh, in_specs=in_specs, out_specs=out_specs, check_vma=False)
+    general = functools.partial(gathered_local, cuts)
+
+    def run(queries, keys, values, bounds):
+        one_block_each = keys.shape[0] == cuts * ctx * BLK
+        local = tree_local if (cuts, ctx) == (2, 16) and one_block_each else general
+        mapped = jax.shard_map(local, mesh=mesh, in_specs=in_specs, out_specs=out_specs, check_vma=False)
+        return mapped(queries, keys, values, bounds)
+
+    return run

time: 130 us -> 80 us (0.62)
  the two profiles are of different devices: /device:TPU:13 before, /device:TPU:27 now
where the time goes in v1:
time: 80 us; the launch traced here: 80.8 us
  Pallas kernels  30.7 us (38%)
  waiting for transfers between devices  24.7 us (31%)
  starting transfers between devices  14.3 us (18%)
  local copies, waits for them, and re-layouts  7.95 us (10%)
  between operations  2.57 us (3%)
    pallas_call x1, Pallas kernels, attention(): pl.pallas_call(functools.partial(attention_kernel, slot_of, sources), gri...  19.7 us
    ppermute x4, waiting for transfers between devices, move(): return lax.ppermute(array, 'ctx', pairs)  12.6 us
    ppermute x4, starting transfers between devices, move(): return lax.ppermute(array, 'ctx', pairs)  8.55 us
    pallas_call x3, Pallas kernels, pick(): pl.pallas_call(functools.partial(pick_kernel, rule, len(arrays)), grid_sp...  8.26 us
    ppermute x1, waiting for transfers between devices, tree_local(): other = lax.ppermute(other, 'cuts', [(0, 1), (1, 0)])  6.14 us
    unnamed x20, local copies, waits for them, and re-layouts  5.79 us
    ppermute x1, waiting for transfers between devices, tree_local(): far_x = lax.ppermute(forward, 'ctx', across)  4.45 us
    pallas_call x1, Pallas kernels, halves(): pl.pallas_call(halves_kernel, grid_spec=grid_spec, out_shape=[shape] * 2,...  2.71 us
  transfers between devices with their start and end apart: 13, of which 5 were waited for; matrix products, arithmetic and copies ran while one was open for 3% of the time, Pallas kernels for 3%

profile of v1, /device:TPU:27, one launch (start us, length us, event | category | flops | bytes accessed | tf_op | source)
XLA Modules:
  0.0 80.8 jit_solution(7174984530008759534)
XLA Ops:
  0.6 2.7 %halves.1 = (bf16[1,2,128,512]{3,2,1,0:T(8,128)(2,1)}, bf16[1,2,128,512]{3,2,1,0:T(8,128)(2,1)}) custom-call(s32[2]{0:T(128)} %pad_add_fusion.place_ref, bf16[128,1024]{1,0:T(8,128)(2,1)} %keys_ref.1, bf16[128,1024]{1,0:T(8,128)(2,1)} %values_ref.1), custom_call_target="tpu_custom_call" | custom-call | tf_op jit(solution)/shard_map/halves/pallas_call | solution.py:206
  3.3 1.3 %collective-permute-start.1 = (bf16[1,2,128,512]{3,2,1,0:T(8,128)(2,1)}, bf16[1,2,128,512]{3,2,1,0:T(8,128)(2,1)S(1)}, u32[]{:S(2)}, u32[]{:S(2)}) collective-permute-start(bf16[1,2,128,512]{3,2,1,0:T(8,128)(2,1)} %get-tuple-element.23), channel_id=1, source_target_pairs={{0,16},{16,0},{1,17},{17,1},{2,18},{18,2},{3,19},{19,3},{4,20},{20... | collective-permute-start | bytes 786440 | tf_op jit(solution)/shard_map/ppermute | solution.py:269
  4.6 6.1 %collective-permute-done.1.refs_1_ = bf16[1,2,128,512]{3,2,1,0:T(8,128)(2,1)S(1)} collective-permute-done((bf16[1,2,128,512]{3,2,1,0:T(8,128)(2,1)}, bf16[1,2,128,512]{3,2,1,0:T(8,128)(2,1)S(1)}, u32[]{:S(2)}, u32[]{:S(2)}) %collective-permute-start.1) | collective-permute-done | bytes 262176 | tf_op jit(solution)/shard_map/ppermute | solution.py:269
  11.4 2.6 %pick.3 = (bf16[1,2,128,512]{3,2,1,0:T(8,128)(2,1)S(1)}, bf16[1,2,128,512]{3,2,1,0:T(8,128)(2,1)}, bf16[1,2,128,512]{3,2,1,0:T(8,128)(2,1)}) custom-call(s32[2]{0:T(128)} %pad_add_fusion.place_ref, s32[3,32]{1,0:T(4,128)} %bounds_ref.7, bf16[1,2,128,512]{3,2,1,0:T(8,128)(2,1)} %get-tuple-element.22.refs_0_, bf16[1,2,128,512]{3,2,1,0:T(8,128)(2,1)} %copy-done.8), custom_call_target="tpu_custom_call" | custom-call | tf_op jit(solution)/shard_map/pick/pallas_call | solution.py:174
  14.1 2.0 %collective-permute-start.4 = (bf16[1,2,128,512]{3,2,1,0:T(8,128)(2,1)}, bf16[1,2,128,512]{3,2,1,0:T(8,128)(2,1)S(1)}, u32[]{:S(2)}, u32[]{:S(2)}) collective-permute-start(bf16[1,2,128,512]{3,2,1,0:T(8,128)(2,1)} %get-tuple-element.26), channel_id=1, source_target_pairs={{12,4},{13,5},{14,6},{15,7},{0,8},{1,9},{2,10},{3,11},{7,15},{28,2... | collective-permute-start | bytes 786440 | tf_op jit(solution)/shard_map/ppermute | solution.py:273
  16.1 1.3 %collective-permute-start.3 = (bf16[1,2,128,512]{3,2,1,0:T(8,128)(2,1)}, bf16[1,2,128,512]{3,2,1,0:T(8,128)(2,1)S(1)}, u32[]{:S(2)}, u32[]{:S(2)}) collective-permute-start(bf16[1,2,128,512]{3,2,1,0:T(8,128)(2,1)} %get-tuple-element.25.refs_1_), channel_id=1, source_target_pairs={{0,4},{1,5},{2,6},{3,7},{4,8},{5,9},{6,10},{7,11},{8,12},{9,13},{1... | collective-permute-start | bytes 786440 | tf_op jit(solution)/shard_map/ppermute | solution.py:273
  17.4 4.0 %collective-permute-start.2 = (bf16[1,2,128,512]{3,2,1,0:T(8,128)(2,1)S(1)}, bf16[1,2,128,512]{3,2,1,0:T(8,128)(2,1)S(1)}, u32[]{:S(2)}, u32[]{:S(2)}) collective-permute-start(bf16[1,2,128,512]{3,2,1,0:T(8,128)(2,1)S(1)} %get-tuple-element.24.refs_0_), channel_id=1, source_target_pairs={{4,0},{5,1},{6,2},{7,3},{8,4},{9,5},{10,6},{11,7},{12,8},{13,9},{1... | collective-permute-start | bytes 786440 | tf_op jit(solution)/shard_map/ppermute | solution.py:273
  21.4 9.2 %collective-permute-done.4.refs_4_ = bf16[1,2,128,512]{3,2,1,0:T(8,128)(2,1)S(1)} collective-permute-done((bf16[1,2,128,512]{3,2,1,0:T(8,128)(2,1)}, bf16[1,2,128,512]{3,2,1,0:T(8,128)(2,1)S(1)}, u32[]{:S(2)}, u32[]{:S(2)}) %collective-permute-start.4) | collective-permute-done | bytes 262176 | tf_op jit(solution)/shard_map/ppermute | solution.py:273
  30.5 0.7 copy-done.7
  31.3 0.7 copy-done.6
  32.0 2.9 %pick.4 = (bf16[1,2,128,512]{3,2,1,0:T(8,128)(2,1)}, bf16[1,2,128,512]{3,2,1,0:T(8,128)(2,1)}, bf16[1,2,128,512]{3,2,1,0:T(8,128)(2,1)}, bf16[1,2,128,512]{3,2,1,0:T(8,128)(2,1)}) custom-call(s32[2]{0:T(128)} %pad_add_fusion.place_ref, s32[3,32]{1,0:T(4,128)} %bounds_ref.7, bf16[1,2,128,512]{3,2,1,0:T(8,128)(2,1)S(1)} %get-tuple-element.24.refs_0_, ...), custom_call_target="tpu_custom_call" | custom-call | tf_op jit(solution)/shard_map/pick/pallas_call | solution.py:174
  35.0 1.3 %collective-permute-start.6 = (bf16[1,2,128,512]{3,2,1,0:T(8,128)(2,1)}, bf16[1,2,128,512]{3,2,1,0:T(8,128)(2,1)S(1)}, u32[]{:S(2)}, u32[]{:S(2)}) collective-permute-start(bf16[1,2,128,512]{3,2,1,0:T(8,128)(2,1)} %get-tuple-element.29), channel_id=1, source_target_pairs={{4,8},{5,9},{6,10},{7,11},{8,12},{9,13},{10,14},{11,15},{20,24},{2... | collective-permute-start | bytes 786440 | tf_op jit(solution)/shard_map/ppermute | solution.py:273
  36.3 1.3 %collective-permute-start.7 = (bf16[1,2,128,512]{3,2,1,0:T(8,128)(2,1)}, bf16[1,2,128,512]{3,2,1,0:T(8,128)(2,1)S(1)}, u32[]{:S(2)}, u32[]{:S(2)}) collective-permute-start(bf16[1,2,128,512]{3,2,1,0:T(8,128)(2,1)} %get-tuple-element.30), channel_id=1, source_target_pairs={{7,5},{11,9},{15,13},{23,21},{27,25},{31,29}} | collective-permute-start | bytes 786440 | tf_op jit(solution)/shard_map/ppermute | solution.py:287
  37.6 1.5 %fusion = (s32[1,1]{1,0:T(1,128)}, s32[1,1]{1,0:T(1,128)}, s32[1,1]{1,0:T(1,128)}) fusion(s32[3,32]{1,0:T(4,128)} %bounds_ref.7), kind=kLoop, calls=%fused_computation.1 | loop fusion | bytes 24 | tf_op jit(solution)/shard_map/slice | solution.py:282
  41.5 3.4 %collective-permute-done.6.refs_5_ = bf16[1,2,128,512]{3,2,1,0:T(8,128)(2,1)S(1)} collective-permute-done((bf16[1,2,128,512]{3,2,1,0:T(8,128)(2,1)}, bf16[1,2,128,512]{3,2,1,0:T(8,128)(2,1)S(1)}, u32[]{:S(2)}, u32[]{:S(2)}) %collective-permute-start.6) | collective-permute-done | bytes 262176 | tf_op jit(solution)/shard_map/ppermute | solution.py:273
  45.6 0.7 copy-done.9
  46.4 2.7 %pick.5 = (bf16[1,2,128,512]{3,2,1,0:T(8,128)(2,1)}, bf16[1,2,128,512]{3,2,1,0:T(8,128)(2,1)}, bf16[1,2,128,512]{3,2,1,0:T(8,128)(2,1)}) custom-call(s32[2]{0:T(128)} %pad_add_fusion.place_ref, s32[3,32]{1,0:T(4,128)} %bounds_ref.7, bf16[1,2,128,512]{3,2,1,0:T(8,128)(2,1)S(1)} %get-tuple-element.24.refs_0_, bf16[1,2,128,512]{3,2,1,0:T(8,128)(2,1)} %copy-done.6, ...), custom_call_target="tpu_custom_call" | custom-call | tf_op jit(solution)/shard_map/pick/pallas_call | solution.py:174
  49.7 2.3 %collective-permute-start.13 = (bf16[1,2,128,512]{3,2,1,0:T(8,128)(2,1)}, bf16[1,2,128,512]{3,2,1,0:T(8,128)(2,1)S(1)}, u32[]{:S(2)}, u32[]{:S(2)}) collective-permute-start(bf16[1,2,128,512]{3,2,1,0:T(8,128)(2,1)} %get-tuple-element.33.refs_8_), channel_id=1, source_target_pairs={{1,0},{3,2},{5,4},{7,6},{9,8},{11,10},{13,12},{15,14},{17,16},{19,... | collective-permute-start | bytes 786440 | tf_op jit(solution)/shard_map/ppermute | solution.py:292
  52.2 4.4 %collective-permute-done.8.refs_3_ = bf16[1,2,128,512]{3,2,1,0:T(8,128)(2,1)S(1)} collective-permute-done((bf16[1,2,128,512]{3,2,1,0:T(8,128)(2,1)}, bf16[1,2,128,512]{3,2,1,0:T(8,128)(2,1)S(1)}, u32[]{:S(2)}, u32[]{:S(2)}) %collective-permute-start.8) | collective-permute-done | bytes 262176 | tf_op jit(solution)/shard_map/ppermute | solution.py:291
  56.7 1.5 %collective-permute-done.12.refs_7_ = bf16[1,2,128,512]{3,2,1,0:T(8,128)(2,1)S(1)} collective-permute-done((bf16[1,2,128,512]{3,2,1,0:T(8,128)(2,1)S(1)}, bf16[1,2,128,512]{3,2,1,0:T(8,128)(2,1)S(1)}, u32[]{:S(2)}, u32[]{:S(2)}) %collective-permute-start.12) | collective-permute-done | bytes 262176 | tf_op jit(solution)/shard_map/ppermute | solution.py:294
  58.2 0.9 %copy-done = bf16[1,2,128,512]{3,2,1,0:T(8,128)(2,1)S(1)} copy-done((bf16[1,2,128,512]{3,2,1,0:T(8,128)(2,1)S(1)}, bf16[1,2,128,512]{3,2,1,0:T(8,128)(2,1)}, u32[]{:S(2)}) %copy-start) | copy-done | bytes 262168
  59.1 0.9 %copy-done.1 = bf16[1,2,128,512]{3,2,1,0:T(8,128)(2,1)S(1)} copy-done((bf16[1,2,128,512]{3,2,1,0:T(8,128)(2,1)S(1)}, bf16[1,2,128,512]{3,2,1,0:T(8,128)(2,1)}, u32[]{:S(2)}) %copy-start.1) | copy-done | bytes 262168
  60.1 0.9 %copy-done.2 = bf16[1,2,128,512]{3,2,1,0:T(8,128)(2,1)S(1)} copy-done((bf16[1,2,128,512]{3,2,1,0:T(8,128)(2,1)S(1)}, bf16[1,2,128,512]{3,2,1,0:T(8,128)(2,1)}, u32[]{:S(2)}) %copy-start.2) | copy-done | bytes 262168
  61.0 19.7 %attention.1 = bf16[256,4096]{1,0:T(8,128)(2,1)} custom-call(s32[2]{0:T(128)S(1)} %copy-done.4, s32[3,32]{1,0:T(4,128)S(1)} %copy-done.3, bf16[256,8192]{1,0:T(8,128)(2,1)} %query_ref.1, bf16[1,2,128,512]{3,2,1,0:T(8,128)(2,1)S(1)} %copy-done, bf16[1,2,128,512]{3,2,1,0:T(8,128)(2,1)S(1)} %collective-permute-done.5.refs_1_, ...), custom_call_target="tpu_custom_call" | custom-call | tf_op jit(solution)/shard_map/attention/pallas_call | solution.py:107
  (31 shorter events, 3.6 us)
Async XLA Ops:
  0.0 58.2 %copy-start.3 = (s32[3,32]{1,0:T(4,128)S(1)}, s32[3,32]{1,0:T(4,128)}, u32[]{:S(2)}) copy-start(s32[3,32]{1,0:T(4,128)} %bounds_ref.7) | copy-start | bytes 1156
  0.6 57.6 %copy-start.4 = (s32[2]{0:T(128)S(1)}, s32[2]{0:T(128)}, u32[]{:S(2)}) copy-start(s32[2]{0:T(128)} %pad_add_fusion.place_ref) | copy-start | bytes 28
  3.3 7.5 %collective-permute-start.1 = (bf16[1,2,128,512]{3,2,1,0:T(8,128)(2,1)}, bf16[1,2,128,512]{3,2,1,0:T(8,128)(2,1)S(1)}, u32[]{:S(2)}, u32[]{:S(2)}) collective-permute-start(bf16[1,2,128,512]{3,2,1,0:T(8,128)(2,1)} %get-tuple-element.23), channel_id=1, source_target_pairs={{0,16},{16,0},{1,17},{17,1},{2,18},{18,2},{3,19},{19,3},{4,20},{20... | collective-permute-start | bytes 786440 | tf_op jit(solution)/shard_map/ppermute | solution.py:269
  10.7 0.7 copy-start.8
  14.1 16.4 %collective-permute-start.4 = (bf16[1,2,128,512]{3,2,1,0:T(8,128)(2,1)}, bf16[1,2,128,512]{3,2,1,0:T(8,128)(2,1)S(1)}, u32[]{:S(2)}, u32[]{:S(2)}) collective-permute-start(bf16[1,2,128,512]{3,2,1,0:T(8,128)(2,1)} %get-tuple-element.26), channel_id=1, source_target_pairs={{12,4},{13,5},{14,6},{15,7},{0,8},{1,9},{2,10},{3,11},{7,15},{28,2... | collective-permute-start | bytes 786440 | tf_op jit(solution)/shard_map/ppermute | solution.py:273
  16.1 14.5 %collective-permute-start.3 = (bf16[1,2,128,512]{3,2,1,0:T(8,128)(2,1)}, bf16[1,2,128,512]{3,2,1,0:T(8,128)(2,1)S(1)}, u32[]{:S(2)}, u32[]{:S(2)}) collective-permute-start(bf16[1,2,128,512]{3,2,1,0:T(8,128)(2,1)} %get-tuple-element.25.refs_1_), channel_id=1, source_target_pairs={{0,4},{1,5},{2,6},{3,7},{4,8},{5,9},{6,10},{7,11},{8,12},{9,13},{1... | collective-permute-start | bytes 786440 | tf_op jit(solution)/shard_map/ppermute | solution.py:273
  17.4 13.2 %collective-permute-start.2 = (bf16[1,2,128,512]{3,2,1,0:T(8,128)(2,1)S(1)}, bf16[1,2,128,512]{3,2,1,0:T(8,128)(2,1)S(1)}, u32[]{:S(2)}, u32[]{:S(2)}) collective-permute-start(bf16[1,2,128,512]{3,2,1,0:T(8,128)(2,1)S(1)} %get-tuple-element.24.refs_0_), channel_id=1, source_target_pairs={{4,0},{5,1},{6,2},{7,3},{8,4},{9,5},{10,6},{11,7},{12,8},{13,9},{1... | collective-permute-start | bytes 786440 | tf_op jit(solution)/shard_map/ppermute | solution.py:273
  30.5 0.7 copy-start.7
  30.5 0.8 %copy-start.5 = (bf16[1,2,128,512]{3,2,1,0:T(8,128)(2,1)}, bf16[1,2,128,512]{3,2,1,0:T(8,128)(2,1)S(1)}, u32[]{:S(2)}) copy-start(bf16[1,2,128,512]{3,2,1,0:T(8,128)(2,1)S(1)} %collective-permute-done.3.refs_3_.refs_2_) | copy-start | bytes 786436
  31.3 0.7 copy-start.6
  35.0 10.0 %collective-permute-start.6 = (bf16[1,2,128,512]{3,2,1,0:T(8,128)(2,1)}, bf16[1,2,128,512]{3,2,1,0:T(8,128)(2,1)S(1)}, u32[]{:S(2)}, u32[]{:S(2)}) collective-permute-start(bf16[1,2,128,512]{3,2,1,0:T(8,128)(2,1)} %get-tuple-element.29), channel_id=1, source_target_pairs={{4,8},{5,9},{6,10},{7,11},{8,12},{9,13},{10,14},{11,15},{20,24},{2... | collective-permute-start | bytes 786440 | tf_op jit(solution)/shard_map/ppermute | solution.py:273
  36.3 9.4 %collective-permute-start.7 = (bf16[1,2,128,512]{3,2,1,0:T(8,128)(2,1)}, bf16[1,2,128,512]{3,2,1,0:T(8,128)(2,1)S(1)}, u32[]{:S(2)}, u32[]{:S(2)}) collective-permute-start(bf16[1,2,128,512]{3,2,1,0:T(8,128)(2,1)} %get-tuple-element.30), channel_id=1, source_target_pairs={{7,5},{11,9},{15,13},{23,21},{27,25},{31,29}} | collective-permute-start | bytes 786440 | tf_op jit(solution)/shard_map/ppermute | solution.py:287
  41.5 10.6 %collective-permute-start.5 = (bf16[1,2,128,512]{3,2,1,0:T(8,128)(2,1)}, bf16[1,2,128,512]{3,2,1,0:T(8,128)(2,1)S(1)}, u32[]{:S(2)}, u32[]{:S(2)}) collective-permute-start(bf16[1,2,128,512]{3,2,1,0:T(8,128)(2,1)} %get-tuple-element.28.refs_4_), channel_id=1, source_target_pairs={{0,2},{1,3},{2,0},{3,1},{4,6},{5,7},{6,4},{7,5},{8,10},{9,11},{10,... | collective-permute-start | bytes 786440 | tf_op jit(solution)/shard_map/ppermute | solution.py:286
  45.6 0.7 copy-start.9
  49.1 7.5 %collective-permute-start.8 = (bf16[1,2,128,512]{3,2,1,0:T(8,128)(2,1)}, bf16[1,2,128,512]{3,2,1,0:T(8,128)(2,1)S(1)}, u32[]{:S(2)}, u32[]{:S(2)}) collective-permute-start(bf16[1,2,128,512]{3,2,1,0:T(8,128)(2,1)} %get-tuple-element.32), channel_id=1, source_target_pairs={{0,2},{1,3},{2,0},{3,1},{4,6},{5,7},{6,4},{7,5},{8,10},{9,11},{10,... | collective-permute-start | bytes 786440 | tf_op jit(solution)/shard_map/ppermute | solution.py:291
  49.2 7.5 %collective-permute-start.9 = (bf16[1,2,128,512]{3,2,1,0:T(8,128)(2,1)}, bf16[1,2,128,512]{3,2,1,0:T(8,128)(2,1)S(1)}, u32[]{:S(2)}, u32[]{:S(2)}) collective-permute-start(bf16[1,2,128,512]{3,2,1,0:T(8,128)(2,1)} %get-tuple-element.27.refs_3_.refs_0_), channel_id=1, source_target_pairs={{0,1},{1,0},{2,3},{3,2},{4,5},{5,4},{6,7},{7,6},{8,9},{9,8},{10,11... | collective-permute-start | bytes 786440 | tf_op jit(solution)/shard_map/ppermute | solution.py:294
  49.7 7.0 %collective-permute-start.11 = (bf16[1,2,128,512]{3,2,1,0:T(8,128)(2,1)}, bf16[1,2,128,512]{3,2,1,0:T(8,128)(2,1)S(1)}, u32[]{:S(2)}, u32[]{:S(2)}) collective-permute-start(bf16[1,2,128,512]{3,2,1,0:T(8,128)(2,1)} %get-tuple-element.31.refs_2_), channel_id=1, source_target_pairs={{0,1},{1,0},{2,3},{3,2},{4,5},{5,4},{6,7},{7,6},{8,9},{9,8},{10,11... | collective-permute-start | bytes 786440 | tf_op jit(solution)/shard_map/ppermute | solution.py:294
  49.7 6.9 %collective-permute-start.13 = (bf16[1,2,128,512]{3,2,1,0:T(8,128)(2,1)}, bf16[1,2,128,512]{3,2,1,0:T(8,128)(2,1)S(1)}, u32[]{:S(2)}, u32[]{:S(2)}) collective-permute-start(bf16[1,2,128,512]{3,2,1,0:T(8,128)(2,1)} %get-tuple-element.33.refs_8_), channel_id=1, source_target_pairs={{1,0},{3,2},{5,4},{7,6},{9,8},{11,10},{13,12},{15,14},{17,16},{19,... | collective-permute-start | bytes 786440 | tf_op jit(solution)/shard_map/ppermute | solution.py:292
  52.1 4.6 %collective-permute-start.10 = (bf16[1,2,128,512]{3,2,1,0:T(8,128)(2,1)S(1)}, bf16[1,2,128,512]{3,2,1,0:T(8,128)(2,1)S(1)}, u32[]{:S(2)}, u32[]{:S(2)}) collective-permute-start(bf16[1,2,128,512]{3,2,1,0:T(8,128)(2,1)S(1)} %collective-permute-done.5.refs_1_), channel_id=1, source_target_pairs={{0,1},{1,0},{2,3},{3,2},{4,5},{5,4},{6,7},{7,6},{8,9},{9,8},{10,11... | collective-permute-start | bytes 786440 | tf_op jit(solution)/shard_map/ppermute | solution.py:294
  56.6 1.5 %collective-permute-start.12 = (bf16[1,2,128,512]{3,2,1,0:T(8,128)(2,1)S(1)}, bf16[1,2,128,512]{3,2,1,0:T(8,128)(2,1)S(1)}, u32[]{:S(2)}, u32[]{:S(2)}) collective-permute-start(bf16[1,2,128,512]{3,2,1,0:T(8,128)(2,1)S(1)} %collective-permute-done.8.refs_3_), channel_id=1, source_target_pairs={{0,1},{1,0},{2,3},{3,2},{4,5},{5,4},{6,7},{7,6},{8,9},{9,8},{10,11... | collective-permute-start | bytes 786440 | tf_op jit(solution)/shard_map/ppermute | solution.py:294
  58.2 1.0 %copy-start = (bf16[1,2,128,512]{3,2,1,0:T(8,128)(2,1)S(1)}, bf16[1,2,128,512]{3,2,1,0:T(8,128)(2,1)}, u32[]{:S(2)}) copy-start(bf16[1,2,128,512]{3,2,1,0:T(8,128)(2,1)} %get-tuple-element.27.refs_3_.refs_0_) | copy-start | bytes 786436
  59.1 0.9 %copy-start.1 = (bf16[1,2,128,512]{3,2,1,0:T(8,128)(2,1)S(1)}, bf16[1,2,128,512]{3,2,1,0:T(8,128)(2,1)}, u32[]{:S(2)}) copy-start(bf16[1,2,128,512]{3,2,1,0:T(8,128)(2,1)} %get-tuple-element.31.refs_2_) | copy-start | bytes 786436
  60.1 0.9 %copy-start.2 = (bf16[1,2,128,512]{3,2,1,0:T(8,128)(2,1)S(1)}, bf16[1,2,128,512]{3,2,1,0:T(8,128)(2,1)}, u32[]{:S(2)}) copy-start(bf16[1,2,128,512]{3,2,1,0:T(8,128)(2,1)} %get-tuple-element.33.refs_8_) | copy-start | bytes 786436
